TPU v7x, 32 devices: a whole 2x2x4 slice. The times are simulated.
32 devices in a mesh: grp: 2 (over y), ka: 16 (over z, x, core).
Axes of the slice: x: 2, y: 2, z: 4, core: 2. Of those that a mesh axis runs over, the one named last changes fastest.
Arguments:
- eigvecs: bfloat16 [16, 2, 64, 1024], P('ka'), may hold values from -0.25 to 0.25
- eigvals: bfloat16 [496, 2, 512], P('ka'), may hold values from -2 to 2
- kpoints: bfloat16 [3, 496], P(None, 'ka'), may hold values from 0 to 1
- counts: int32 [16], P('ka'), may hold values from 1 to 31, as said below
- energy_real: float32 [2], P('grp'), parts along dimension 0, may hold values from -0.5 to 0.5
- energy_imag: float32 [2], P('grp'), parts along dimension 0, may hold values from 0.1 to 0.4
- offsets: int32 [3, 16], replicated, may hold values from -4 to 4, as said below
- atom_orbitals: int32 [8], replicated, may hold values from 1 to 12, 64 in all
- positions: float32 [3, 8], replicated, may hold values from 0 to 1
- exch_split: float32 [64, 64], replicated, may hold values from -6 to 6
Outputs:
- exchange: float32 [32, 8, 8], P(('grp', 'ka')), parts along dimension 0
There are 2 independent parts, one for each index of `grp`. A program takes and returns all parts, laid end to end along the dimension named above; an argument that names none is the same for every part. Nothing has to cross between parts.
Inputs may be any that keep to these rules, and one draw needn't show every extreme that they name: For every device d below the axis's middle, counts[d] + counts[d + 8] is at most 32, one of the two exceeds 16, and the pair of device 0 reaches the maximum count. `offsets`: for r < 8, column r + 8 is minus column r, and the first component of column r is 1 to 4.
All inputs are finite; a program needn't handle non-finite values.
Results may differ from a plain program's by a relative error of at most 0.0063.
The roundings to bfloat16 on the way count: a program that leaves them out, or rounds other values in their place, can miss the bound.
Values may be sent and summed in bfloat16 or wider, within the bound.
A program may use at most 128 MiB of HBM per device.

v0:
```python
import jax
import jax.numpy as jnp
from jax import lax
from jax.sharding import PartitionSpec as P

inv_four_pi = 0.25 / 3.141592653589793
two_pi = 2.0 * 3.141592653589793


def member_table(atom_orbitals, mag):
    ends = jnp.cumsum(atom_orbitals)
    starts = ends - atom_orbitals
    orbital = jnp.arange(mag, dtype=jnp.int32)[:, None]
    return ((orbital >= starts[None, :]) & (orbital < ends[None, :])).astype(jnp.float32)


def scale_rows(vectors, levels, energy_real, energy_imag):
    norb = levels.shape[-1]
    levels_wide = levels.astype(jnp.float32)
    shift = energy_real[0] - levels_wide
    denom = shift * shift + energy_imag[0] * energy_imag[0]
    real_factor = (shift / denom)[:, :, None, :]
    imag_factor = (-energy_imag[0] / denom)[:, :, None, :]
    wide = vectors.astype(jnp.float32)
    re_vec = wide[..., :norb]
    im_vec = wide[..., norb:]
    scaled = jnp.concatenate(
        [re_vec * real_factor - im_vec * imag_factor, re_vec * imag_factor + im_vec * real_factor],
        -1,
    ).astype(jnp.bfloat16)
    right = jnp.concatenate(
        [vectors, jnp.concatenate([-vectors[..., norb:], vectors[..., :norb]], -1)], axis=-2
    )
    return (scaled, right)


def shared_green(vectors, levels, energy_real, energy_imag):
    scaled, right = scale_rows(vectors, levels, energy_real, energy_imag)
    return jnp.einsum("ksan,scn->ksac", scaled, right, preferred_element_type=jnp.float32)


def apply_gauge(product, coords, site):
    mag = site.shape[1]
    kpos = jnp.einsum(
        "xk,xa->ka", coords.astype(jnp.float32), site, precision=lax.Precision.HIGHEST
    )
    phase = two_pi * (kpos[:, None, :] - kpos[:, :, None])
    cos_phase = jnp.cos(phase)[:, None]
    sin_phase = jnp.sin(phase)[:, None]
    green_re = product[..., :mag]
    green_im = product[..., mag:]
    new_re = green_re * cos_phase - green_im * sin_phase
    new_im = green_re * sin_phase + green_im * cos_phase
    stacked = jnp.stack([new_re, new_im], axis=2)
    return stacked.reshape(product.shape[0], 2, 2, mag * mag).astype(jnp.bfloat16)


def phase_terms(coords, slot_weights, lattice, grid):
    angle = two_pi * jnp.einsum(
        "ck,cr->rk",
        coords.astype(jnp.float32),
        lattice.astype(jnp.float32),
        precision=lax.Precision.HIGHEST,
    )
    weight_wide = slot_weights.astype(jnp.float32)[None, :]
    cos_weight = (jnp.cos(angle) * weight_wide).astype(jnp.bfloat16)
    sin_weight = (jnp.sin(angle) * weight_wide).astype(jnp.bfloat16)

    def matmul(left, right):
        return jnp.dot(left, right, preferred_element_type=jnp.float32)

    def combine(sign, spin):
        real_sum = matmul(cos_weight, grid[:, spin, 0]) + sign * matmul(
            sin_weight, grid[:, spin, 1]
        )
        imag_sum = matmul(cos_weight, grid[:, spin, 1]) - sign * matmul(
            sin_weight, grid[:, spin, 0]
        )
        return [real_sum, imag_sum]

    pieces = combine(1.0, 0) + combine(1.0, 1)
    pieces = pieces + combine(-1.0, 1)
    return jnp.concatenate(pieces, axis=1)


def pair_exchange(up_block, down_block, exch_split, member):
    mag = exch_split.shape[0]
    rows = up_block.shape[0]
    area = mag * mag
    up_re = up_block[:, :area].reshape(rows, mag, mag)
    up_im = up_block[:, area:].reshape(rows, mag, mag)
    down_re = down_block[:, :area].reshape(rows, mag, mag)
    down_im = down_block[:, area:].reshape(rows, mag, mag)
    same_atom = jnp.dot(member, member.T, precision=lax.Precision.HIGHEST)
    splitting = 0.5 * (exch_split + exch_split.T) * same_atom
    high = lax.Precision.HIGHEST
    left_re = jnp.einsum("ab,rbc->rac", splitting, up_re, precision=high)
    left_im = jnp.einsum("ab,rbc->rac", splitting, up_im, precision=high)
    right_re = jnp.einsum("ab,rbc->rac", splitting, down_re, precision=high)
    right_im = jnp.einsum("ab,rbc->rac", splitting, down_im, precision=high)
    im_part = left_re * jnp.swapaxes(right_im, 1, 2) + left_im * jnp.swapaxes(right_re, 1, 2)
    return -inv_four_pi * jnp.einsum("ai,rab,bj->rij", member, im_part, member, precision=high)


def local(
    eigvecs,
    eigvals,
    kpoints,
    counts,
    energy_real,
    energy_imag,
    offsets,
    atom_orbitals,
    positions,
    exch_split,
):
    kslot = eigvals.shape[0]
    mag = eigvecs.shape[2]
    area = mag * mag
    member = member_table(atom_orbitals, mag)
    site = jnp.dot(positions, member.T, precision=lax.Precision.HIGHEST)
    count_here = counts[0]
    slot_index = jnp.arange(kslot, dtype=jnp.int32)
    inverse = (1.0 / count_here.astype(jnp.float32)).astype(jnp.bfloat16)
    weights = jnp.where(slot_index < count_here, inverse, jnp.zeros((), jnp.bfloat16))
    coords, slot_weights = (kpoints, weights)
    product = shared_green(eigvecs[0], eigvals, energy_real, energy_imag)
    grid = apply_gauge(product, coords, site)
    owned = lax.psum_scatter(
        phase_terms(coords, slot_weights, offsets, grid), "ka", scatter_dimension=0, tiled=True
    )
    mirror_block = owned[:, 4 * area :]
    return pair_exchange(owned[:, : 2 * area], mirror_block, exch_split, member)


def solution(mesh):
    placed = (
        P("ka", None, None, None),
        P("ka", None, None),
        P(None, "ka"),
        P("ka"),
        P("grp"),
        P("grp"),
        P(),
        P(),
        P(),
        P(),
    )
    return jax.shard_map(
        local, mesh=mesh, in_specs=placed, out_specs=P(("grp", "ka"), None, None), check_vma=False
    )
```

profile of v0, /device:TPU:0, one launch (start us, length us, event | category | flops | bytes accessed | tf_op | source)
XLA Modules:
  0.0 134.7 jit_solution(9919144526543984787)
XLA Ops:
  7.9 1.0 fusion.27
  8.9 1.0 bitcast_convert_fusion
  10.0 0.2 reduce-window.8
  10.4 0.2 convolution_bitcast_fusion.4
  10.6 3.6 %fusion.15 = (f32[31,64,64]{2,1,0:T(8,128)S(1)}, f32[31,64,64]{2,1,0:T(8,128)S(1)}) fusion(f32[31,64]{1,0:T(8,128)S(1)} %convolution_bitcast_fusion.4), kind=kLoop, calls=%fused_computation.28 | loop fusion | flops 253952 | bytes 1023744 | tf_op jit(solution)/shard_map/cos | solution.py:48
  14.2 2.7 %subtract_convert_fusion = (bf16[31,2,64,512]{3,2,0,1:T(8,128)(2,1)S(1)}, bf16[31,2,64,512]{3,2,0,1:T(8,128)(2,1)S(1)}) fusion(f32[31,2,512]{2,0,1:T(8,128)S(1)} %copy.22, f32[2,64,512]{2,1,0:T(8,128)S(1)} %get-tuple-element.14, f32[31,2,512]{2,0,1:T(8,128)S(1)} %copy.21, f32[2,64,512]{2,1,0:T(8,128)S(1)} %get-tuple-element.13), kind=kLoop, calls=%fused_computation.5 | loop fusion | flops 16252928 | bytes 8904704 | tf_op jit(solution)/shard_map/convert.4
  16.9 2.5 %fusion.6 = f32[31,2,64,128]{3,2,0,1:T(8,128)S(1)} fusion(bf16[31,2,64,512]{3,2,0,1:T(8,128)(2,1)S(1)} %get-tuple-element.12, bf16[31,2,64,512]{3,2,0,1:T(8,128)(2,1)S(1)} %get-tuple-element.11, bf16[2,64,512]{2,1,0:T(8,128)(2,1)S(1)} %get-tuple-element.16, bf16[2,64,512]{2,1,0:T(8,128)(2,1)S(1)} %get-tuple-element.15, bf16[2,64,1024]{2,1,0:T(8,128)(2,1)S(1)} %bitcast.103), kind=kOutput, calls=%fused_computation.12 | convolution fusion | flops 1058013184 | bytes 10682368 | tf_op jit(solution)/shard_map/ksan,scn->ksac/dot_general | solution.py:39
  19.4 0.8 add_convert_fusion.1
  20.2 0.9 stack.7
  21.8 0.9 stack.8
  22.7 0.2 multiply_convert_fusion
  23.6 0.2 fusion.5
  23.8 0.2 fusion.4
  24.0 0.2 add_dynamic-update-slice_fusion.1
  24.2 0.2 subtract_dynamic-update-slice_fusion.1
  24.4 1.1 copy-done.1
  25.7 0.6 dynamic-slice
  26.4 97.4 %all-reduce.3.cloned.1.call-done = f32[16,24576]{1,0:T(8,128)} async-done(((f32[16,24576]{1,0:T(8,128)}), f32[16,24576]{1,0:T(8,128)}) %all-reduce.3.cloned.1.call-update) | async-done | bytes 1572880
  123.8 2.0 %dynamic-slice_reduce_fusion.3 = (f32[4096]{0:T(1024)S(1)}, f32[4096]{0:T(1024)S(1)}, f32[4096]{0:T(1024)S(1)}, f32[4096]{0:T(1024)S(1)}) fusion(f32[16,24576]{1,0:T(8,128)} %all-reduce.3.cloned.1.call-done, u32[]{:T(128)} %bitcast.25, u32[]{:T(128)S(6)} %convert.19, u32[]{:T(128)S(6)} %convert.18, u32[]{:T(128)S(6)} %convert.20), kind=kLoop, calls=%fused_computation.61 | loop fusion | bytes 131088 | tf_op jit(solution)/shard_map/slice | solution.py:90
  126.0 0.2 convolution_bitcast_fusion
  126.4 0.2 fusion.12
  126.7 0.2 fusion.11
  126.9 0.2 fusion.31
  127.1 0.8 fusion.13
  (37 shorter events, 1.7 us)
Async XLA Ops:
  6.5 3.7 %copy-start = (f32[3,8]{1,0:T(4,128)S(1)}, f32[3,8]{1,0:T(4,128)}, u32[]{:S(2)}) copy-start(f32[3,8]{1,0:T(4,128)} %param.18) | copy-start | bytes 292
  6.5 3.5 %copy-start.2 = (bf16[1,2,64,1024]{3,2,1,0:T(8,128)(2,1)S(1)}, bf16[1,2,64,1024]{3,2,1,0:T(8,128)(2,1)}, u32[]{:S(2)}) copy-start(bf16[1,2,64,1024]{3,2,1,0:T(8,128)(2,1)} %param.10) | copy-start | bytes 786436
  6.5 3.5 %copy-start.6 = (s32[8]{0:T(128)S(1)}, s32[8]{0:T(128)}, u32[]{:S(2)}) copy-start(s32[8]{0:T(128)} %param.17) | copy-start | bytes 100
  6.5 3.8 %copy-start.5 = (bf16[3,31]{1,0:T(4,128)(2,1)S(1)}, bf16[3,31]{1,0:T(4,128)(2,1)}, u32[]{:S(2)}) copy-start(bf16[3,31]{1,0:T(4,128)(2,1)} %param.12) | copy-start | bytes 562
  6.5 117.3 %all-reduce.3.cloned.1.call-start = ((), (), s32[]{:S(2)}) async-start(), calls=%async_computation | async-start | bytes 3145728
  20.2 2.5 %copy-start.4 = (s32[3,16]{1,0:T(4,128)S(1)}, s32[3,16]{1,0:T(4,128)}, u32[]{:S(2)}) copy-start(s32[3,16]{1,0:T(4,128)} %param.16) | copy-start | bytes 580
  24.1 1.5 %copy-start.3 = (f32[64,64]{1,0:T(8,128)S(1)}, f32[64,64]{1,0:T(8,128)}, u32[]{:S(2)}) copy-start(f32[64,64]{1,0:T(8,128)} %param.19) | copy-start | bytes 49156
  24.2 1.5 %copy-start.7 = (u32[32]{0:T(128)S(1)}, u32[32]{0:T(128)}, u32[]{:S(2)}) copy-start(u32[32]{0:T(128)} %constant.25) | copy-start | bytes 388
  24.4 1.2 copy-start.1
Sparse Core Ops, SparseCore 0:
  25.7 98.0 all-reduce.2
where the time goes:
time: 135 us
  waiting for transfers between devices  97.4 us (72%)
  between operations  15.7 us (12%)
  other arithmetic  9.35 us (7%)
  matrix products  6.24 us (5%)
  local copies, waits for them, and re-layouts  5.93 us (4%)
    unnamed x2, waiting for transfers between devices  97.4 us
    another operation x3, other arithmetic  3.7 us
    cos x1, other arithmetic, apply_gauge(): cos_phase = jnp.cos(phase)[:, None]  3.61 us
  transfers between devices with their start and end apart: 1, of which 1 were waited for; matrix products, arithmetic and copies ran while one was open for 1% of the time, Pallas kernels for 0%

commit v1 on v0

v1 whole, which is shorter than its diff:
```python
import functools

import jax
import jax.numpy as jnp
from jax import lax
from jax.experimental import pallas as pl
from jax.experimental.pallas import tpu as pltpu
from jax.sharding import PartitionSpec as P

inv_four_pi = 0.25 / 3.141592653589793
two_pi = 2.0 * 3.141592653589793

ROWS = 16
HIGH = lax.Precision.HIGHEST
ACROSS = (((1,), (1,)), ((), ()))


def wave(turns):
    part = (turns - jnp.round(turns)) * two_pi
    return jnp.cos(part), jnp.sin(part)


def one_hot(condition):
    return jnp.where(condition, 1.0, 0.0).astype(jnp.bfloat16)


def iota(shape, axis):
    return lax.broadcasted_iota(jnp.int32, shape, axis)


def kernel(
    n,
    vec_ref,
    lev_ref,
    k_ref,
    count_ref,
    er_ref,
    ei_ref,
    off_ref,
    orb_ref,
    pos_ref,
    split_ref,
    out_ref,
    vf,
    right,
    levels,
    fre,
    fim,
    ctab,
    stab,
    wbd,
    scaled,
    acc,
    acc2,
    acc3,
    send1,
    recv1,
    send2,
    recv2,
    send3,
    recv3,
    ssem1,
    rsem1,
    ssem2,
    rsem2,
    ssem3,
    rsem3,
):
    mag, norb = vec_ref.shape[2], vec_ref.shape[3] // 2
    kslot = lev_ref.shape[0]
    slots = levels.shape[1]
    atoms = orb_ref.shape[0]
    blocks = mag // ROWS
    chunks = 2 * blocks
    quarter, eighth = n // 4, n // 8
    wide = 2 * mag

    me = lax.axis_index("ka")
    b0, b1, q = lax.rem(me, 2), lax.rem(me // 2, 2), me // 4
    mate0 = {"ka": me + 1 - 2 * b0}
    mate1 = {"ka": me + 2 - 4 * b1}

    def peer(k):
        return lax.rem(q + k, quarter)

    def peer_id(k):
        return {"ka": peer(k) * 4 + b1 * 2 + b0}

    barrier = pltpu.get_barrier_semaphore()
    for other in [mate0, mate1] + [peer_id(k) for k in range(1, quarter)]:
        pl.semaphore_signal(
            barrier, inc=1, device_id=other, device_id_type=pl.DeviceIdType.MESH
        )

    for spin in range(2):
        vectors = vec_ref[0, spin]
        vf[spin] = vectors.astype(jnp.float32)
        right[spin, :mag, :] = vectors
        right[spin, mag:, :norb] = -vectors[:, norb:]
        right[spin, mag:, norb:] = vectors[:, :norb]
        levels[spin] = jnp.zeros((slots, norb), jnp.float32)
    for s in range(kslot):
        row = lev_ref[s].astype(jnp.float32)
        levels[0, s : s + 1, :] = row[0:1]
        levels[1, s : s + 1, :] = row[1:2]
    er, ei = er_ref[0], ei_ref[0]
    for spin in range(2):
        shift = er - levels[spin]
        denom = shift * shift + ei * ei
        inverse = 1.0 / denom
        fre[spin] = shift * inverse
        fim[spin] = -ei * inverse

    lane = iota((1, wide), 1)
    lane = jnp.where(lane >= mag, lane - mag, lane)
    down_rows = iota((mag, 1), 0)
    id_row = jnp.zeros((1, wide), jnp.int32)
    id_col = jnp.zeros((mag, 1), jnp.int32)
    end = jnp.int32(0)
    for i in range(atoms):
        end = end + orb_ref[i]
        id_row = id_row + jnp.where(lane >= end, 1, 0)
        id_col = id_col + jnp.where(down_rows >= end, 1, 0)

    coords = k_ref[...]
    eye = one_hot(iota((slots, kslot), 0) == iota((slots, kslot), 1))
    k_cols = lax.dot_general(eye, coords, ACROSS, preferred_element_type=jnp.float32)
    kpos = jnp.zeros((slots, wide), jnp.float32)
    for x in range(3):
        site = jnp.zeros((1, wide), jnp.float32)
        for i in range(atoms):
            site = jnp.where(id_row == i, pos_ref[x, i], site)
        kpos = kpos + k_cols[:, x : x + 1] * site
    cos_c, sin_c = wave(kpos)
    sign = jnp.where(iota((1, wide), 1) < mag, -1.0, 1.0)
    cos_s, sin_s = cos_c * sign, sin_c * sign
    for a in range(mag):
        cos_a, sin_a = cos_c[:, a : a + 1], sin_c[:, a : a + 1]
        ctab[a * slots : (a + 1) * slots, :] = cos_c * cos_a + sin_c * sin_a
        stab[a * slots : (a + 1) * slots, :] = sin_s * cos_a - cos_s * sin_a

    half = n // 2
    ordered = iota((half, n), 0)
    wanted = (
        lax.rem(ordered, eighth) * 4
        + lax.rem(ordered // eighth, 2) * 2
        + ordered // quarter
    )
    pick = one_hot(wanted == iota((half, n), 1))
    lattice = off_ref[...].astype(jnp.float32).astype(jnp.bfloat16)
    off_cols = lax.dot_general(pick, lattice, ACROSS, preferred_element_type=jnp.float32)
    spread = one_hot(iota((kslot, slots), 0) == iota((kslot, slots), 1))
    k_rows = jnp.dot(coords, spread, preferred_element_type=jnp.float32)
    turns = jnp.zeros((half, slots), jnp.float32)
    for x in range(3):
        turns = turns + off_cols[:, x : x + 1] * k_rows[x : x + 1, :]
    cos_t, sin_t = wave(turns)
    count = jnp.full((1, slots), count_ref[0], jnp.int32)
    weight = (1.0 / count.astype(jnp.float32)).astype(jnp.bfloat16).astype(jnp.float32)
    weight = jnp.where(iota((1, slots), 1) < count, weight, 0.0)
    table = jnp.concatenate([cos_t * weight, sin_t * weight], 0).astype(jnp.bfloat16)
    deep = 8 * slots
    rows_of = one_hot(iota((8 * n, n), 0) // 8 == iota((8 * n, n), 1))
    tall = jnp.dot(rows_of, table, preferred_element_type=jnp.float32).astype(jnp.bfloat16)
    lanes_of = one_hot(iota((slots, deep), 0) == lax.rem(iota((slots, deep), 1), slots))
    full = jnp.dot(tall, lanes_of, preferred_element_type=jnp.float32)
    own = lax.rem(iota((8 * n, deep), 0), 8) == iota((8 * n, deep), 1) // slots
    wbd[...] = jnp.where(own, full, 0.0).astype(jnp.bfloat16)

    pl.semaphore_wait(barrier, quarter + 1)

    def compute(c):
        spin, start = c // blocks, lax.rem(c, blocks) * ROWS
        f_re, f_im = fre[spin], fim[spin]
        for j in range(ROWS):
            v = vf[spin, pl.ds(start + j, 1), :]
            v_re, v_im = v[:, :norb], v[:, norb:]
            band = slice(j * slots, (j + 1) * slots)
            scaled[band, :norb] = (v_re * f_re - v_im * f_im).astype(jnp.bfloat16)
            scaled[band, norb:] = (v_re * f_im + v_im * f_re).astype(jnp.bfloat16)
        bare = lax.dot_general(
            scaled[...], right[spin], ACROSS, preferred_element_type=jnp.float32
        )
        here = pl.ds(pl.multiple_of(start * slots, ROWS * slots), ROWS * slots)
        green = bare * ctab[here, :] + pltpu.roll(bare, mag, 1) * stab[here, :]
        green = green.astype(jnp.bfloat16)
        sense = jnp.where(spin == 0, 1.0, -1.0) * -sign
        for part in range(ROWS // 8):
            mixed = jnp.dot(
                wbd[...], green[part * deep : (part + 1) * deep], preferred_element_type=jnp.float32
            )
            even = mixed[: 4 * n].reshape(2, 2, eighth, 8, wide)
            odd = (pltpu.roll(mixed[4 * n :], mag, 1) * sense).reshape(2, 2, eighth, 8, wide)
            rows = slice(part * 8, part * 8 + 8)
            acc[c, :, :, :eighth, rows, :] = even + odd
            acc[c, :, :, eighth:, rows, :] = even - odd

    def copy1(c):
        return pltpu.make_async_remote_copy(
            src_ref=send1.at[c],
            dst_ref=recv1.at[c],
            send_sem=ssem1.at[c],
            recv_sem=rsem1.at[c],
            device_id=mate0,
            device_id_type=pl.DeviceIdType.MESH,
        )

    def copy2(c):
        return pltpu.make_async_remote_copy(
            src_ref=send2.at[c],
            dst_ref=recv2.at[c],
            send_sem=ssem2.at[c],
            recv_sem=rsem2.at[c],
            device_id=mate1,
            device_id_type=pl.DeviceIdType.MESH,
        )

    def copy3(c, k):
        return pltpu.make_async_remote_copy(
            src_ref=send3.at[c, peer(k)],
            dst_ref=recv3.at[c, k - 1],
            send_sem=ssem3.at[c, k - 1],
            recv_sem=rsem3.at[c, k - 1],
            device_id=peer_id(k),
            device_id_type=pl.DeviceIdType.MESH,
        )

    def stage1(c):
        send1[c] = acc[c, 1 - b0].astype(jnp.bfloat16)
        copy1(c).start()

    def stage2(c):
        copy1(c).wait()
        passed = acc[c, b0, 1 - b1] + recv1[c, 1 - b1].astype(jnp.float32)
        send2[c] = passed.astype(jnp.bfloat16)
        copy2(c).start()
        acc2[c] = acc[c, b0, b1] + recv1[c, b1].astype(jnp.float32)

    def stage3(c):
        copy2(c).wait()
        total = acc2[c] + recv2[c].astype(jnp.float32)
        send3[c] = total.astype(jnp.bfloat16)
        for k in range(1, quarter):
            copy3(c, k).start()
        acc2[c] = total
        acc3[c] = acc2[c, q]

    def step(c, carry):
        compute(c)
        stage1(c)

        @pl.when(c >= 1)
        def _():
            stage2(c - 1)

        @pl.when(c >= 2)
        def _():
            stage3(c - 2)

        return carry

    lax.fori_loop(0, chunks, step, 0)
    stage2(chunks - 1)
    stage3(chunks - 2)
    stage3(chunks - 1)

    same = id_col == id_row[:, :mag]
    split = split_ref[...]
    splitting = jnp.where(same, 0.5 * (split + split.T), 0.0)
    member_rows = jnp.where(iota((atoms, mag), 0) == id_row[:, :mag], 1.0, 0.0)
    member_cols = jnp.where(id_col == iota((mag, atoms), 1), 1.0, 0.0)

    def landed(c, carry):
        for k in range(1, quarter):
            copy3(c, k).wait()
        total = acc3[c]
        for k in range(1, quarter):
            total = total + recv3[c, k - 1].astype(jnp.float32)
        acc3[c] = total
        return carry

    lax.fori_loop(0, chunks, landed, 0)
    up = acc3[:blocks].reshape(mag, wide)
    down = acc3[blocks:].reshape(mag, wide)
    left = jnp.dot(splitting, up, precision=HIGH, preferred_element_type=jnp.float32)
    turned = jnp.dot(down.T, splitting, precision=HIGH, preferred_element_type=jnp.float32)
    im_part = left[:, :mag] * turned[mag:] + left[:, mag:] * turned[:mag]
    by_atom = jnp.dot(member_rows, im_part, precision=HIGH, preferred_element_type=jnp.float32)
    pairs = jnp.dot(by_atom, member_cols, precision=HIGH, preferred_element_type=jnp.float32)
    out_ref[0] = -inv_four_pi * pairs


def local(n, *args):
    eigvecs, eigvals, offsets, atom_orbitals = args[0], args[1], args[6], args[7]
    mag, norb = eigvecs.shape[2], eigvals.shape[2]
    slots = -(-eigvals.shape[0] // 16) * 16
    atoms = atom_orbitals.shape[0]
    chunks = 2 * mag // ROWS
    quarter = n // 4
    wide = 2 * mag
    assert offsets.shape[1] == n and n % 8 == 0 and mag % ROWS == 0
    vmem = pl.BlockSpec(memory_space=pltpu.VMEM)
    smem = pl.BlockSpec(memory_space=pltpu.SMEM)
    f32, bf16 = jnp.float32, jnp.bfloat16
    tile = (ROWS, wide)
    dma = pltpu.SemaphoreType.DMA
    return pl.pallas_call(
        functools.partial(kernel, n),
        out_shape=jax.ShapeDtypeStruct((1, atoms, atoms), f32),
        in_specs=[vmem, vmem, vmem, smem, smem, smem, vmem, smem, smem, vmem],
        out_specs=vmem,
        scratch_shapes=[
            pltpu.VMEM((2, mag, 2 * norb), f32),
            pltpu.VMEM((2, wide, 2 * norb), bf16),
            pltpu.VMEM((2, slots, norb), f32),
            pltpu.VMEM((2, slots, norb), f32),
            pltpu.VMEM((2, slots, norb), f32),
            pltpu.VMEM((mag * slots, wide), f32),
            pltpu.VMEM((mag * slots, wide), f32),
            pltpu.VMEM((8 * n, 8 * slots), bf16),
            pltpu.VMEM((ROWS * slots, 2 * norb), bf16),
            pltpu.VMEM((chunks, 2, 2, quarter) + tile, f32),
            pltpu.VMEM((chunks, quarter) + tile, f32),
            pltpu.VMEM((chunks,) + tile, f32),
            pltpu.VMEM((chunks, 2, quarter) + tile, bf16),
            pltpu.VMEM((chunks, 2, quarter) + tile, bf16),
            pltpu.VMEM((chunks, quarter) + tile, bf16),
            pltpu.VMEM((chunks, quarter) + tile, bf16),
            pltpu.VMEM((chunks, quarter) + tile, bf16),
            pltpu.VMEM((chunks, quarter - 1) + tile, bf16),
            dma((chunks,)),
            dma((chunks,)),
            dma((chunks,)),
            dma((chunks,)),
            dma((chunks, quarter - 1)),
            dma((chunks, quarter - 1)),
        ],
        compiler_params=pltpu.CompilerParams(
            collective_id=0, has_side_effects=True, vmem_limit_bytes=48 * 1024 * 1024
        ),
    )(*args)


def solution(mesh):
    placed = (
        P("ka", None, None, None),
        P("ka", None, None),
        P(None, "ka"),
        P("ka"),
        P("grp"),
        P("grp"),
        P(),
        P(),
        P(),
        P(),
    )
    return jax.shard_map(
        functools.partial(local, mesh.shape["ka"]),
        mesh=mesh,
        in_specs=placed,
        out_specs=P(("grp", "ka"), None, None),
        check_vma=False,
    )
```

time: 135 us -> 31.6 us (0.23)
  waiting for transfers between devices: 97.4 us -> 0 us
  Pallas kernels: 0 us -> 26.1 us
  between operations: 15.7 us -> 2.06 us
  other arithmetic: 9.35 us -> 0 us
  matrix products: 6.24 us -> 0 us
  local copies, waits for them, and re-layouts: 5.93 us -> 3.15 us
    unnamed x2 -> x0, waiting for transfers between devices: 97.4 us -> none
    pallas_call x0 -> x1, Pallas kernels: none -> 26.1 us  [local(): pl.pallas_call(functools.partial(kernel, n), out_shape=jax.ShapeDtypeStru...]
    dot_general x19 -> x0, matrix products: 6.24 us -> none  [the longest x1 2.48 us: shared_green(): jnp.einsum('ksan,scn->ksac', scaled, right, preferred_element_type=jnp.fl...]
    another operation x3 -> x0, other arithmetic: 3.7 us -> none
    cos x1 -> x0, other arithmetic: 3.61 us -> none  [apply_gauge(): cos_phase = jnp.cos(phase)[:, None]]
    another operation x6 -> x0, local copies, waits for them, and re-layouts: 2.03 us -> none  [the longest x2 1.74 us: apply_gauge(): stacked = jnp.stack([new_re, new_im], axis=2)]
    slice x2 -> x0, local copies, waits for them, and re-layouts: 2.01 us -> none  [the longest x1 1.97 us: pair_exchange(): up_re = up_block[:, :area].reshape(rows, mag, mag)]
    unnamed x18 -> x15, local copies, waits for them, and re-layouts: 1.85 us -> 3.15 us
  transfers between devices with their start and end apart: 1 -> 0, of which waited for: 1 -> 0; matrix products, arithmetic and copies ran while one was open for 1% -> 0% of each run, Pallas kernels for 0% -> 0%
where the time goes in v1:
time: 31.6 us; the launch traced here: 31.3 us
  Pallas kernels  26.1 us (83%)
  local copies, waits for them, and re-layouts  3.15 us (10%)
  between operations  2.06 us (7%)
    pallas_call x1, Pallas kernels, local(): pl.pallas_call(functools.partial(kernel, n), out_shape=jax.ShapeDtypeStru...  26.1 us
    unnamed x15, local copies, waits for them, and re-layouts  3.15 us

profile of v1, /device:TPU:0, one launch (start us, length us, event | category | flops | bytes accessed | tf_op | source)
XLA Modules:
  0.0 31.3 jit_solution(14066636948746229437)
XLA Ops:
  0.0 0.0 copy-start.4
  0.7 0.0 copy-start.3
  1.3 0.0 copy-start.5
  1.3 0.0 copy-start.6
  2.0 0.0 copy-done.4
  2.0 0.0 copy-done.3
  2.0 0.0 copy-done.5
  2.1 0.0 copy-done.6
  2.1 0.0 copy-start
  2.1 0.9 %copy-done = bf16[1,2,64,1024]{3,2,1,0:T(8,128)(2,1)S(1)} copy-done((bf16[1,2,64,1024]{3,2,1,0:T(8,128)(2,1)S(1)}, bf16[1,2,64,1024]{3,2,1,0:T(8,128)(2,1)}, u32[]{:S(2)}) %copy-start) | copy-done | bytes 262168
  3.0 0.0 copy-start.1
  3.0 0.8 %copy-done.1 = bf16[31,2,512]{2,1,0:T(2,128)(2,1)S(1)} copy-done((bf16[31,2,512]{2,1,0:T(2,128)(2,1)S(1)}, bf16[31,2,512]{2,1,0:T(2,128)(2,1)}, u32[]{:S(2)}) %copy-start.1) | copy-done | bytes 63512
  3.8 0.0 copy-start.2
  3.8 0.8 %copy-done.2 = f32[64,64]{1,0:T(8,128)S(1)} copy-done((f32[64,64]{1,0:T(8,128)S(1)}, f32[64,64]{1,0:T(8,128)}, u32[]{:S(2)}) %copy-start.2) | copy-done | bytes 16408
  4.6 26.1 %shard_map.100 = f32[1,8,8]{2,1,0:T(8,128)S(1)} custom-call(bf16[1,2,64,1024]{3,2,1,0:T(8,128)(2,1)S(1)} %copy-done, bf16[31,2,512]{2,1,0:T(2,128)(2,1)S(1)} %copy-done.1, bf16[3,31]{1,0:T(4,128)(2,1)S(1)} %copy-done.5, s32[1]{0:T(128)S(6)} %copy.12.count_ref, f32[1]{0:T(128)S(6)} %copy.13.er_ref, f32[1]{0:T(128)S(6)} %copy.14.ei_ref, ...), custom_call_target="tpu_custom_call" | custom-call | tf_op jit(solution)/shard_map/pallas_call | solution.py:307
  30.7 0.6 %copy.15 = f32[1,8,8]{2,1,0:T(8,128)} copy(f32[1,8,8]{2,1,0:T(8,128)S(1)} %shard_map.100) | data formatting | bytes 512
Async XLA Ops:
  0.0 2.0 %copy-start.4 = (f32[3,8]{1,0:T(4,128)S(1)}, f32[3,8]{1,0:T(4,128)}, u32[]{:S(2)}) copy-start(f32[3,8]{1,0:T(4,128)} %pos_ref.1) | copy-start | bytes 292
  0.7 1.4 %copy-start.3 = (s32[3,16]{1,0:T(4,128)S(1)}, s32[3,16]{1,0:T(4,128)}, u32[]{:S(2)}) copy-start(s32[3,16]{1,0:T(4,128)} %off_ref.1) | copy-start | bytes 580
  1.3 0.7 %copy-start.5 = (bf16[3,31]{1,0:T(4,128)(2,1)S(1)}, bf16[3,31]{1,0:T(4,128)(2,1)}, u32[]{:S(2)}) copy-start(bf16[3,31]{1,0:T(4,128)(2,1)} %k_ref.1) | copy-start | bytes 562
  1.3 0.7 %copy-start.6 = (s32[8]{0:T(128)S(1)}, s32[8]{0:T(128)}, u32[]{:S(2)}) copy-start(s32[8]{0:T(128)} %orb_ref.1) | copy-start | bytes 100
  2.1 1.0 %copy-start = (bf16[1,2,64,1024]{3,2,1,0:T(8,128)(2,1)S(1)}, bf16[1,2,64,1024]{3,2,1,0:T(8,128)(2,1)}, u32[]{:S(2)}) copy-start(bf16[1,2,64,1024]{3,2,1,0:T(8,128)(2,1)} %vec_ref.1) | copy-start | bytes 786436
  3.0 0.8 %copy-start.1 = (bf16[31,2,512]{2,1,0:T(2,128)(2,1)S(1)}, bf16[31,2,512]{2,1,0:T(2,128)(2,1)}, u32[]{:S(2)}) copy-start(bf16[31,2,512]{2,1,0:T(2,128)(2,1)} %lev_ref.1) | copy-start | bytes 190468
  3.8 0.8 %copy-start.2 = (f32[64,64]{1,0:T(8,128)S(1)}, f32[64,64]{1,0:T(8,128)}, u32[]{:S(2)}) copy-start(f32[64,64]{1,0:T(8,128)} %split_ref.1) | copy-start | bytes 49156

commit v2 on v1

--- a/solution.py
+++ b/solution.py
@@ -30,6 +30,18 @@
 
 def kernel(
     n,
+    groups,
+    vec_hbm,
+    lev_hbm,
+    k_hbm,
+    count_hbm,
+    er_hbm,
+    ei_hbm,
+    off_hbm,
+    orb_hbm,
+    pos_hbm,
+    split_hbm,
+    out_ref,
     vec_ref,
     lev_ref,
     k_ref,
@@ -40,9 +52,9 @@
     orb_ref,
     pos_ref,
     split_ref,
-    out_ref,
     vf,
     right,
+    flipped,
     levels,
     fre,
     fim,
@@ -59,6 +71,7 @@
     recv2,
     send3,
     recv3,
+    isem,
     ssem1,
     rsem1,
     ssem2,
@@ -66,12 +79,31 @@
     ssem3,
     rsem3,
 ):
+    fetches = [
+        pltpu.make_async_copy(source, target, isem.at[i])
+        for i, (source, target) in enumerate(
+            [
+                (vec_hbm, vec_ref),
+                (lev_hbm, lev_ref),
+                (er_hbm, er_ref),
+                (ei_hbm, ei_ref),
+                (k_hbm, k_ref),
+                (orb_hbm, orb_ref),
+                (pos_hbm, pos_ref),
+                (off_hbm, off_ref),
+                (count_hbm, count_ref),
+                (split_hbm, split_ref),
+            ]
+        )
+    ]
+    for fetch in fetches:
+        fetch.start()
+
     mag, norb = vec_ref.shape[2], vec_ref.shape[3] // 2
     kslot = lev_ref.shape[0]
     slots = levels.shape[1]
     atoms = orb_ref.shape[0]
     blocks = mag // ROWS
-    chunks = 2 * blocks
     quarter, eighth = n // 4, n // 8
     wide = 2 * mag
 
@@ -91,25 +123,39 @@
         pl.semaphore_signal(
             barrier, inc=1, device_id=other, device_id_type=pl.DeviceIdType.MESH
         )
-
-    for spin in range(2):
-        vectors = vec_ref[0, spin]
-        vf[spin] = vectors.astype(jnp.float32)
-        right[spin, :mag, :] = vectors
-        right[spin, mag:, :norb] = -vectors[:, norb:]
-        right[spin, mag:, norb:] = vectors[:, :norb]
-        levels[spin] = jnp.zeros((slots, norb), jnp.float32)
+    for fetch in fetches:
+        fetch.wait()
+
     for s in range(kslot):
         row = lev_ref[s].astype(jnp.float32)
         levels[0, s : s + 1, :] = row[0:1]
         levels[1, s : s + 1, :] = row[1:2]
     er, ei = er_ref[0], ei_ref[0]
     for spin in range(2):
+        levels[spin, kslot:, :] = jnp.zeros((slots - kslot, norb), jnp.float32)
+        vectors = vec_ref[0, spin]
+        vf[spin] = vectors.astype(jnp.float32)
+        right[spin, :mag, :] = vectors
+        right[spin, mag:, :norb] = -vectors[:, norb:]
+        right[spin, mag:, norb:] = vectors[:, :norb]
+        flipped[spin] = right[spin].T
         shift = er - levels[spin]
         denom = shift * shift + ei * ei
         inverse = 1.0 / denom
         fre[spin] = shift * inverse
         fim[spin] = -ei * inverse
+
+    def scale(i):
+        spin, start = i // blocks, i % blocks * ROWS
+        f_re, f_im = fre[spin], fim[spin]
+        for j in range(ROWS):
+            v = vf[spin, start + j : start + j + 1, :]
+            v_re, v_im = v[:, :norb], v[:, norb:]
+            band = slice(j * slots, (j + 1) * slots)
+            scaled[i % 2, band, :norb] = (v_re * f_re - v_im * f_im).astype(jnp.bfloat16)
+            scaled[i % 2, band, norb:] = (v_re * f_im + v_im * f_re).astype(jnp.bfloat16)
+
+    scale(0)
 
     lane = iota((1, wide), 1)
     lane = jnp.where(lane >= mag, lane - mag, lane)
@@ -167,24 +213,19 @@
     own = lax.rem(iota((8 * n, deep), 0), 8) == iota((8 * n, deep), 1) // slots
     wbd[...] = jnp.where(own, full, 0.0).astype(jnp.bfloat16)
 
-    pl.semaphore_wait(barrier, quarter + 1)
-
-    def compute(c):
-        spin, start = c // blocks, lax.rem(c, blocks) * ROWS
-        f_re, f_im = fre[spin], fim[spin]
-        for j in range(ROWS):
-            v = vf[spin, pl.ds(start + j, 1), :]
-            v_re, v_im = v[:, :norb], v[:, norb:]
-            band = slice(j * slots, (j + 1) * slots)
-            scaled[band, :norb] = (v_re * f_re - v_im * f_im).astype(jnp.bfloat16)
-            scaled[band, norb:] = (v_re * f_im + v_im * f_re).astype(jnp.bfloat16)
-        bare = lax.dot_general(
-            scaled[...], right[spin], ACROSS, preferred_element_type=jnp.float32
-        )
-        here = pl.ds(pl.multiple_of(start * slots, ROWS * slots), ROWS * slots)
+    same = id_col == id_row[:, :mag]
+    split = split_ref[...]
+    splitting = jnp.where(same, 0.5 * (split + split.T), 0.0)
+    member_rows = jnp.where(iota((atoms, mag), 0) == id_row[:, :mag], 1.0, 0.0)
+    member_cols = jnp.where(id_col == iota((mag, atoms), 1), 1.0, 0.0)
+
+    def mix(i):
+        spin, start = i // blocks, i % blocks * ROWS
+        bare = jnp.dot(scaled[i % 2], flipped[spin], preferred_element_type=jnp.float32)
+        here = slice(start * slots, (start + ROWS) * slots)
         green = bare * ctab[here, :] + pltpu.roll(bare, mag, 1) * stab[here, :]
         green = green.astype(jnp.bfloat16)
-        sense = jnp.where(spin == 0, 1.0, -1.0) * -sign
+        sense = sign if spin else -sign
         for part in range(ROWS // 8):
             mixed = jnp.dot(
                 wbd[...], green[part * deep : (part + 1) * deep], preferred_element_type=jnp.float32
@@ -192,97 +233,98 @@
             even = mixed[: 4 * n].reshape(2, 2, eighth, 8, wide)
             odd = (pltpu.roll(mixed[4 * n :], mag, 1) * sense).reshape(2, 2, eighth, 8, wide)
             rows = slice(part * 8, part * 8 + 8)
-            acc[c, :, :, :eighth, rows, :] = even + odd
-            acc[c, :, :, eighth:, rows, :] = even - odd
-
-    def copy1(c):
+            acc[i, :, :, :eighth, rows, :] = even + odd
+            acc[i, :, :, eighth:, rows, :] = even - odd
+
+    def span(g):
+        return pl.ds(groups[g][0], groups[g][1])
+
+    def copy1(g):
         return pltpu.make_async_remote_copy(
-            src_ref=send1.at[c],
-            dst_ref=recv1.at[c],
-            send_sem=ssem1.at[c],
-            recv_sem=rsem1.at[c],
+            src_ref=send1.at[span(g)],
+            dst_ref=recv1.at[span(g)],
+            send_sem=ssem1.at[g],
+            recv_sem=rsem1.at[g],
             device_id=mate0,
             device_id_type=pl.DeviceIdType.MESH,
         )
 
-    def copy2(c):
+    def copy2(g):
         return pltpu.make_async_remote_copy(
-            src_ref=send2.at[c],
-            dst_ref=recv2.at[c],
-            send_sem=ssem2.at[c],
-            recv_sem=rsem2.at[c],
+            src_ref=send2.at[span(g)],
+            dst_ref=recv2.at[span(g)],
+            send_sem=ssem2.at[g],
+            recv_sem=rsem2.at[g],
             device_id=mate1,
             device_id_type=pl.DeviceIdType.MESH,
         )
 
-    def copy3(c, k):
+    def copy3(g, k):
         return pltpu.make_async_remote_copy(
-            src_ref=send3.at[c, peer(k)],
-            dst_ref=recv3.at[c, k - 1],
-            send_sem=ssem3.at[c, k - 1],
-            recv_sem=rsem3.at[c, k - 1],
+            src_ref=send3.at[peer(k), span(g)],
+            dst_ref=recv3.at[k - 1, span(g)],
+            send_sem=ssem3.at[g, k - 1],
+            recv_sem=rsem3.at[g, k - 1],
             device_id=peer_id(k),
             device_id_type=pl.DeviceIdType.MESH,
         )
 
-    def stage1(c):
-        send1[c] = acc[c, 1 - b0].astype(jnp.bfloat16)
-        copy1(c).start()
-
-    def stage2(c):
-        copy1(c).wait()
-        passed = acc[c, b0, 1 - b1] + recv1[c, 1 - b1].astype(jnp.float32)
-        send2[c] = passed.astype(jnp.bfloat16)
-        copy2(c).start()
-        acc2[c] = acc[c, b0, b1] + recv1[c, b1].astype(jnp.float32)
-
-    def stage3(c):
-        copy2(c).wait()
-        total = acc2[c] + recv2[c].astype(jnp.float32)
-        send3[c] = total.astype(jnp.bfloat16)
+    def members(g):
+        return range(groups[g][0], groups[g][0] + groups[g][1])
+
+    def stage1(g):
+        if g == 0:
+            pl.semaphore_wait(barrier, quarter + 1)
+        for i in members(g):
+            send1[i] = acc[i, 1 - b0].astype(jnp.bfloat16)
+        copy1(g).start()
+
+    def stage2(g):
+        copy1(g).wait()
+        for i in members(g):
+            passed = acc[i, b0, 1 - b1] + recv1[i, 1 - b1].astype(jnp.float32)
+            send2[i] = passed.astype(jnp.bfloat16)
+        copy2(g).start()
+        for i in members(g):
+            acc2[i] = acc[i, b0, b1] + recv1[i, b1].astype(jnp.float32)
+
+    def stage3(g):
+        copy2(g).wait()
+        for i in members(g):
+            total = acc2[i] + recv2[i].astype(jnp.float32)
+            send3[:, i] = total.astype(jnp.bfloat16)
+            acc2[i] = total
         for k in range(1, quarter):
-            copy3(c, k).start()
-        acc2[c] = total
-        acc3[c] = acc2[c, q]
-
-    def step(c, carry):
-        compute(c)
-        stage1(c)
-
-        @pl.when(c >= 1)
-        def _():
-            stage2(c - 1)
-
-        @pl.when(c >= 2)
-        def _():
-            stage3(c - 2)
-
-        return carry
-
-    lax.fori_loop(0, chunks, step, 0)
-    stage2(chunks - 1)
-    stage3(chunks - 2)
-    stage3(chunks - 1)
-
-    same = id_col == id_row[:, :mag]
-    split = split_ref[...]
-    splitting = jnp.where(same, 0.5 * (split + split.T), 0.0)
-    member_rows = jnp.where(iota((atoms, mag), 0) == id_row[:, :mag], 1.0, 0.0)
-    member_cols = jnp.where(id_col == iota((mag, atoms), 1), 1.0, 0.0)
-
-    def landed(c, carry):
+            copy3(g, k).start()
+        for i in members(g):
+            acc3[i] = acc2[i, q]
+
+    def stage4(g):
         for k in range(1, quarter):
-            copy3(c, k).wait()
-        total = acc3[c]
-        for k in range(1, quarter):
-            total = total + recv3[c, k - 1].astype(jnp.float32)
-        acc3[c] = total
-        return carry
-
-    lax.fori_loop(0, chunks, landed, 0)
-    up = acc3[:blocks].reshape(mag, wide)
+            copy3(g, k).wait()
+        for i in members(g):
+            total = acc3[i]
+            for k in range(1, quarter):
+                total = total + recv3[k - 1, i].astype(jnp.float32)
+            acc3[i] = total
+
+    due = {}
+    for g, (first, length) in enumerate(groups):
+        for wait, stage in enumerate([stage1, stage2, stage3, stage4]):
+            due.setdefault(first + length - 1 + wait, []).insert(0, (stage, g))
+    left = None
+    for i in range(2 * blocks + 3):
+        if i + 1 < 2 * blocks:
+            scale(i + 1)
+        if i < 2 * blocks:
+            mix(i)
+        for stage, g in due.get(i, []):
+            stage(g)
+        if i == 2 * blocks:
+            up = acc3[:blocks].reshape(mag, wide)
+            left = jnp.dot(splitting, up, precision=HIGH, preferred_element_type=jnp.float32)
+
     down = acc3[blocks:].reshape(mag, wide)
-    left = jnp.dot(splitting, up, precision=HIGH, preferred_element_type=jnp.float32)
     turned = jnp.dot(down.T, splitting, precision=HIGH, preferred_element_type=jnp.float32)
     im_part = left[:, :mag] * turned[mag:] + left[:, mag:] * turned[:mag]
     by_atom = jnp.dot(member_rows, im_part, precision=HIGH, preferred_element_type=jnp.float32)
@@ -299,26 +341,37 @@
     quarter = n // 4
     wide = 2 * mag
     assert offsets.shape[1] == n and n % 8 == 0 and mag % ROWS == 0
-    vmem = pl.BlockSpec(memory_space=pltpu.VMEM)
-    smem = pl.BlockSpec(memory_space=pltpu.SMEM)
+    groups, first = [], 0
+    while first < chunks:
+        length = 2 if chunks - first > 3 else 1
+        groups.append((first, length))
+        first += length
+    sends = len(groups)
     f32, bf16 = jnp.float32, jnp.bfloat16
     tile = (ROWS, wide)
     dma = pltpu.SemaphoreType.DMA
+    on_smem = (3, 4, 5, 7, 8)
+    staged = [
+        (pltpu.SMEM if i in on_smem else pltpu.VMEM)(arg.shape, arg.dtype)
+        for i, arg in enumerate(args)
+    ]
     return pl.pallas_call(
-        functools.partial(kernel, n),
+        functools.partial(kernel, n, groups),
         out_shape=jax.ShapeDtypeStruct((1, atoms, atoms), f32),
-        in_specs=[vmem, vmem, vmem, smem, smem, smem, vmem, smem, smem, vmem],
-        out_specs=vmem,
-        scratch_shapes=[
+        in_specs=[pl.BlockSpec(memory_space=pltpu.HBM)] * len(args),
+        out_specs=pl.BlockSpec(memory_space=pltpu.VMEM),
+        scratch_shapes=staged
+        + [
             pltpu.VMEM((2, mag, 2 * norb), f32),
             pltpu.VMEM((2, wide, 2 * norb), bf16),
+            pltpu.VMEM((2, 2 * norb, wide), bf16),
             pltpu.VMEM((2, slots, norb), f32),
             pltpu.VMEM((2, slots, norb), f32),
             pltpu.VMEM((2, slots, norb), f32),
             pltpu.VMEM((mag * slots, wide), f32),
             pltpu.VMEM((mag * slots, wide), f32),
             pltpu.VMEM((8 * n, 8 * slots), bf16),
-            pltpu.VMEM((ROWS * slots, 2 * norb), bf16),
+            pltpu.VMEM((2, ROWS * slots, 2 * norb), bf16),
             pltpu.VMEM((chunks, 2, 2, quarter) + tile, f32),
             pltpu.VMEM((chunks, quarter) + tile, f32),
             pltpu.VMEM((chunks,) + tile, f32),
@@ -326,14 +379,15 @@
             pltpu.VMEM((chunks, 2, quarter) + tile, bf16),
             pltpu.VMEM((chunks, quarter) + tile, bf16),
             pltpu.VMEM((chunks, quarter) + tile, bf16),
-            pltpu.VMEM((chunks, quarter) + tile, bf16),
-            pltpu.VMEM((chunks, quarter - 1) + tile, bf16),
-            dma((chunks,)),
-            dma((chunks,)),
-            dma((chunks,)),
-            dma((chunks,)),
-            dma((chunks, quarter - 1)),
-            dma((chunks, quarter - 1)),
+            pltpu.VMEM((quarter, chunks) + tile, bf16),
+            pltpu.VMEM((quarter - 1, chunks) + tile, bf16),
+            dma((len(args),)),
+            dma((sends,)),
+            dma((sends,)),
+            dma((sends,)),
+            dma((sends,)),
+            dma((sends, quarter - 1)),
+            dma((sends, quarter - 1)),
         ],
         compiler_params=pltpu.CompilerParams(
             collective_id=0, has_side_effects=True, vmem_limit_bytes=48 * 1024 * 1024

time: 31.6 us -> 33.6 us (1.063)
  Pallas kernels: 26.1 us -> 28 us
    pallas_call x1, Pallas kernels: 26.1 us -> 28 us  [local(): pl.pallas_call(functools.partial(kernel, n, groups), out_shape=jax.ShapeD...]
where the time goes in v2:
time: 33.6 us; the launch traced here: 33.3 us
  Pallas kernels  28 us (83%)
  local copies, waits for them, and re-layouts  3.15 us (9%)
  between operations  2.06 us (6%)
    pallas_call x1, Pallas kernels, local(): pl.pallas_call(functools.partial(kernel, n, groups), out_shape=jax.ShapeD...  28 us
    unnamed x15, local copies, waits for them, and re-layouts  3.15 us

profile of v2, /device:TPU:0, one launch (start us, length us, event | category | flops | bytes accessed | tf_op | source)
XLA Modules:
  0.0 33.3 jit_solution(6814379884534106615)
XLA Ops:
  0.0 0.0 copy-start.4
  0.7 0.0 copy-start.3
  1.3 0.0 copy-start.5
  1.3 0.0 copy-start.6
  2.0 0.0 copy-done.4
  2.0 0.0 copy-done.3
  2.0 0.0 copy-done.5
  2.1 0.0 copy-done.6
  2.1 0.0 copy-start
  2.1 0.9 %copy-done = bf16[1,2,64,1024]{3,2,1,0:T(8,128)(2,1)S(1)} copy-done((bf16[1,2,64,1024]{3,2,1,0:T(8,128)(2,1)S(1)}, bf16[1,2,64,1024]{3,2,1,0:T(8,128)(2,1)}, u32[]{:S(2)}) %copy-start) | copy-done | bytes 262168
  3.0 0.0 copy-start.1
  3.0 0.8 %copy-done.1 = bf16[31,2,512]{2,1,0:T(2,128)(2,1)S(1)} copy-done((bf16[31,2,512]{2,1,0:T(2,128)(2,1)S(1)}, bf16[31,2,512]{2,1,0:T(2,128)(2,1)}, u32[]{:S(2)}) %copy-start.1) | copy-done | bytes 63512
  3.8 0.0 copy-start.2
  3.8 0.8 %copy-done.2 = f32[64,64]{1,0:T(8,128)S(1)} copy-done((f32[64,64]{1,0:T(8,128)S(1)}, f32[64,64]{1,0:T(8,128)}, u32[]{:S(2)}) %copy-start.2) | copy-done | bytes 16408
  4.6 28.0 %shard_map.100 = f32[1,8,8]{2,1,0:T(8,128)S(1)} custom-call(bf16[1,2,64,1024]{3,2,1,0:T(8,128)(2,1)S(1)} %copy-done, bf16[31,2,512]{2,1,0:T(2,128)(2,1)S(1)} %copy-done.1, bf16[3,31]{1,0:T(4,128)(2,1)S(1)} %copy-done.5, s32[1]{0:T(128)S(6)} %copy.12.count_hbm, f32[1]{0:T(128)S(6)} %copy.13.er_hbm, f32[1]{0:T(128)S(6)} %copy.14.ei_hbm, ...), custom_call_target="tpu_custom_call" | custom-call | tf_op jit(solution)/shard_map/pallas_call | solution.py:358
  32.7 0.6 %copy.15 = f32[1,8,8]{2,1,0:T(8,128)} copy(f32[1,8,8]{2,1,0:T(8,128)S(1)} %shard_map.100) | data formatting | bytes 512
Async XLA Ops:
  0.0 2.0 %copy-start.4 = (f32[3,8]{1,0:T(4,128)S(1)}, f32[3,8]{1,0:T(4,128)}, u32[]{:S(2)}) copy-start(f32[3,8]{1,0:T(4,128)} %pos_hbm.1) | copy-start | bytes 292
  0.7 1.4 %copy-start.3 = (s32[3,16]{1,0:T(4,128)S(1)}, s32[3,16]{1,0:T(4,128)}, u32[]{:S(2)}) copy-start(s32[3,16]{1,0:T(4,128)} %off_hbm.1) | copy-start | bytes 580
  1.3 0.7 %copy-start.5 = (bf16[3,31]{1,0:T(4,128)(2,1)S(1)}, bf16[3,31]{1,0:T(4,128)(2,1)}, u32[]{:S(2)}) copy-start(bf16[3,31]{1,0:T(4,128)(2,1)} %k_hbm.1) | copy-start | bytes 562
  1.3 0.7 %copy-start.6 = (s32[8]{0:T(128)S(1)}, s32[8]{0:T(128)}, u32[]{:S(2)}) copy-start(s32[8]{0:T(128)} %orb_hbm.1) | copy-start | bytes 100
  2.1 1.0 %copy-start = (bf16[1,2,64,1024]{3,2,1,0:T(8,128)(2,1)S(1)}, bf16[1,2,64,1024]{3,2,1,0:T(8,128)(2,1)}, u32[]{:S(2)}) copy-start(bf16[1,2,64,1024]{3,2,1,0:T(8,128)(2,1)} %vec_hbm.1) | copy-start | bytes 786436
  3.0 0.8 %copy-start.1 = (bf16[31,2,512]{2,1,0:T(2,128)(2,1)S(1)}, bf16[31,2,512]{2,1,0:T(2,128)(2,1)}, u32[]{:S(2)}) copy-start(bf16[31,2,512]{2,1,0:T(2,128)(2,1)} %lev_hbm.1) | copy-start | bytes 190468
  3.8 0.8 %copy-start.2 = (f32[64,64]{1,0:T(8,128)S(1)}, f32[64,64]{1,0:T(8,128)}, u32[]{:S(2)}) copy-start(f32[64,64]{1,0:T(8,128)} %split_hbm.1) | copy-start | bytes 49156

commit v3 on v2

--- a/solution.py
+++ b/solution.py
@@ -30,7 +30,6 @@
 
 def kernel(
     n,
-    groups,
     vec_hbm,
     lev_hbm,
     k_hbm,
@@ -61,15 +60,14 @@
     ctab,
     stab,
     wbd,
-    scaled,
+    scaled_a,
+    scaled_b,
     acc,
     acc2,
     acc3,
-    send1,
     recv1,
     send2,
     recv2,
-    send3,
     recv3,
     isem,
     ssem1,
@@ -131,7 +129,8 @@
         levels[0, s : s + 1, :] = row[0:1]
         levels[1, s : s + 1, :] = row[1:2]
     er, ei = er_ref[0], ei_ref[0]
-    for spin in range(2):
+
+    def prepare(spin, carry):
         levels[spin, kslot:, :] = jnp.zeros((slots - kslot, norb), jnp.float32)
         vectors = vec_ref[0, spin]
         vf[spin] = vectors.astype(jnp.float32)
@@ -144,18 +143,21 @@
         inverse = 1.0 / denom
         fre[spin] = shift * inverse
         fim[spin] = -ei * inverse
-
-    def scale(i):
-        spin, start = i // blocks, i % blocks * ROWS
+        return carry
+
+    lax.fori_loop(0, 2, prepare, 0)
+
+    def scale(h, scaled):
+        spin, start = h // (2 * blocks), lax.rem(h, 2 * blocks) * 8
         f_re, f_im = fre[spin], fim[spin]
-        for j in range(ROWS):
-            v = vf[spin, start + j : start + j + 1, :]
+        for j in range(8):
+            v = vf[spin, pl.ds(start + j, 1), :]
             v_re, v_im = v[:, :norb], v[:, norb:]
             band = slice(j * slots, (j + 1) * slots)
-            scaled[i % 2, band, :norb] = (v_re * f_re - v_im * f_im).astype(jnp.bfloat16)
-            scaled[i % 2, band, norb:] = (v_re * f_im + v_im * f_re).astype(jnp.bfloat16)
-
-    scale(0)
+            scaled[band, :norb] = (v_re * f_re - v_im * f_im).astype(jnp.bfloat16)
+            scaled[band, norb:] = (v_re * f_im + v_im * f_re).astype(jnp.bfloat16)
+
+    scale(0, scaled_a)
 
     lane = iota((1, wide), 1)
     lane = jnp.where(lane >= mag, lane - mag, lane)
@@ -180,10 +182,19 @@
     cos_c, sin_c = wave(kpos)
     sign = jnp.where(iota((1, wide), 1) < mag, -1.0, 1.0)
     cos_s, sin_s = cos_c * sign, sin_c * sign
-    for a in range(mag):
-        cos_a, sin_a = cos_c[:, a : a + 1], sin_c[:, a : a + 1]
-        ctab[a * slots : (a + 1) * slots, :] = cos_c * cos_a + sin_c * sin_a
-        stab[a * slots : (a + 1) * slots, :] = sin_s * cos_a - cos_s * sin_a
+    deep = 8 * slots
+
+    def gauge(h, carry):
+        cos_r = pltpu.roll(cos_c, wide - 8 * h, 1)
+        sin_r = pltpu.roll(sin_c, wide - 8 * h, 1)
+        for j in range(8):
+            cos_a, sin_a = cos_r[:, j : j + 1], sin_r[:, j : j + 1]
+            here = pl.ds(pl.multiple_of(h * deep + j * slots, slots), slots)
+            ctab[here, :] = cos_c * cos_a + sin_c * sin_a
+            stab[here, :] = sin_s * cos_a - cos_s * sin_a
+        return carry
+
+    lax.fori_loop(0, mag // 8, gauge, 0)
 
     half = n // 2
     ordered = iota((half, n), 0)
@@ -205,7 +216,6 @@
     weight = (1.0 / count.astype(jnp.float32)).astype(jnp.bfloat16).astype(jnp.float32)
     weight = jnp.where(iota((1, slots), 1) < count, weight, 0.0)
     table = jnp.concatenate([cos_t * weight, sin_t * weight], 0).astype(jnp.bfloat16)
-    deep = 8 * slots
     rows_of = one_hot(iota((8 * n, n), 0) // 8 == iota((8 * n, n), 1))
     tall = jnp.dot(rows_of, table, preferred_element_type=jnp.float32).astype(jnp.bfloat16)
     lanes_of = one_hot(iota((slots, deep), 0) == lax.rem(iota((slots, deep), 1), slots))
@@ -219,110 +229,105 @@
     member_rows = jnp.where(iota((atoms, mag), 0) == id_row[:, :mag], 1.0, 0.0)
     member_cols = jnp.where(id_col == iota((mag, atoms), 1), 1.0, 0.0)
 
-    def mix(i):
-        spin, start = i // blocks, i % blocks * ROWS
-        bare = jnp.dot(scaled[i % 2], flipped[spin], preferred_element_type=jnp.float32)
-        here = slice(start * slots, (start + ROWS) * slots)
+    def mix(h, part, scaled):
+        spin, start = h // (2 * blocks), lax.rem(h, 2 * blocks) * deep
+        bare = jnp.dot(scaled[...], flipped[spin], preferred_element_type=jnp.float32)
+        here = pl.ds(pl.multiple_of(start, deep), deep)
         green = bare * ctab[here, :] + pltpu.roll(bare, mag, 1) * stab[here, :]
-        green = green.astype(jnp.bfloat16)
-        sense = sign if spin else -sign
-        for part in range(ROWS // 8):
-            mixed = jnp.dot(
-                wbd[...], green[part * deep : (part + 1) * deep], preferred_element_type=jnp.float32
-            )
-            even = mixed[: 4 * n].reshape(2, 2, eighth, 8, wide)
-            odd = (pltpu.roll(mixed[4 * n :], mag, 1) * sense).reshape(2, 2, eighth, 8, wide)
-            rows = slice(part * 8, part * 8 + 8)
-            acc[i, :, :, :eighth, rows, :] = even + odd
-            acc[i, :, :, eighth:, rows, :] = even - odd
-
-    def span(g):
-        return pl.ds(groups[g][0], groups[g][1])
-
-    def copy1(g):
+        mixed = jnp.dot(
+            wbd[...], green.astype(jnp.bfloat16), preferred_element_type=jnp.float32
+        )
+        sense = jnp.where(spin == 0, 1.0, -1.0) * -sign
+        even = mixed[: 4 * n].reshape(2, 2, eighth, 8, wide)
+        odd = (pltpu.roll(mixed[4 * n :], mag, 1) * sense).reshape(2, 2, eighth, 8, wide)
+        rows = slice(part * 8, part * 8 + 8)
+        c = h // 2
+        acc[c, :, :, :eighth, rows, :] = even + odd
+        acc[c, :, :, eighth:, rows, :] = even - odd
+
+    def copy1(c):
         return pltpu.make_async_remote_copy(
-            src_ref=send1.at[span(g)],
-            dst_ref=recv1.at[span(g)],
-            send_sem=ssem1.at[g],
-            recv_sem=rsem1.at[g],
+            src_ref=acc.at[c, 1 - b0],
+            dst_ref=recv1.at[c],
+            send_sem=ssem1.at[c],
+            recv_sem=rsem1.at[c],
             device_id=mate0,
             device_id_type=pl.DeviceIdType.MESH,
         )
 
-    def copy2(g):
+    def copy2(c):
         return pltpu.make_async_remote_copy(
-            src_ref=send2.at[span(g)],
-            dst_ref=recv2.at[span(g)],
-            send_sem=ssem2.at[g],
-            recv_sem=rsem2.at[g],
+            src_ref=send2.at[c],
+            dst_ref=recv2.at[c],
+            send_sem=ssem2.at[c],
+            recv_sem=rsem2.at[c],
             device_id=mate1,
             device_id_type=pl.DeviceIdType.MESH,
         )
 
-    def copy3(g, k):
+    def copy3(c, k):
         return pltpu.make_async_remote_copy(
-            src_ref=send3.at[peer(k), span(g)],
-            dst_ref=recv3.at[k - 1, span(g)],
-            send_sem=ssem3.at[g, k - 1],
-            recv_sem=rsem3.at[g, k - 1],
+            src_ref=acc2.at[c, peer(k)],
+            dst_ref=recv3.at[c, k - 1],
+            send_sem=ssem3.at[c, k - 1],
+            recv_sem=rsem3.at[c, k - 1],
             device_id=peer_id(k),
             device_id_type=pl.DeviceIdType.MESH,
         )
 
-    def members(g):
-        return range(groups[g][0], groups[g][0] + groups[g][1])
-
-    def stage1(g):
-        if g == 0:
-            pl.semaphore_wait(barrier, quarter + 1)
-        for i in members(g):
-            send1[i] = acc[i, 1 - b0].astype(jnp.bfloat16)
-        copy1(g).start()
-
-    def stage2(g):
-        copy1(g).wait()
-        for i in members(g):
-            passed = acc[i, b0, 1 - b1] + recv1[i, 1 - b1].astype(jnp.float32)
-            send2[i] = passed.astype(jnp.bfloat16)
-        copy2(g).start()
-        for i in members(g):
-            acc2[i] = acc[i, b0, b1] + recv1[i, b1].astype(jnp.float32)
-
-    def stage3(g):
-        copy2(g).wait()
-        for i in members(g):
-            total = acc2[i] + recv2[i].astype(jnp.float32)
-            send3[:, i] = total.astype(jnp.bfloat16)
-            acc2[i] = total
+    def stage1(c):
+        copy1(c).start()
+
+    def stage2(c):
+        copy1(c).wait()
+        send2[c] = acc[c, b0, 1 - b1] + recv1[c, 1 - b1]
+        copy2(c).start()
+        acc2[c] = acc[c, b0, b1] + recv1[c, b1]
+
+    def stage3(c):
+        copy2(c).wait()
+        acc2[c] = acc2[c] + recv2[c]
         for k in range(1, quarter):
-            copy3(g, k).start()
-        for i in members(g):
-            acc3[i] = acc2[i, q]
-
-    def stage4(g):
+            copy3(c, k).start()
+        acc3[c] = acc2[c, q]
+
+    def stage4(c, carry):
         for k in range(1, quarter):
-            copy3(g, k).wait()
-        for i in members(g):
-            total = acc3[i]
-            for k in range(1, quarter):
-                total = total + recv3[k - 1, i].astype(jnp.float32)
-            acc3[i] = total
-
-    due = {}
-    for g, (first, length) in enumerate(groups):
-        for wait, stage in enumerate([stage1, stage2, stage3, stage4]):
-            due.setdefault(first + length - 1 + wait, []).insert(0, (stage, g))
-    left = None
-    for i in range(2 * blocks + 3):
-        if i + 1 < 2 * blocks:
-            scale(i + 1)
-        if i < 2 * blocks:
-            mix(i)
-        for stage, g in due.get(i, []):
-            stage(g)
-        if i == 2 * blocks:
-            up = acc3[:blocks].reshape(mag, wide)
-            left = jnp.dot(splitting, up, precision=HIGH, preferred_element_type=jnp.float32)
+            copy3(c, k).wait()
+        total = acc3[c]
+        for k in range(1, quarter):
+            total = total + recv3[c, k - 1]
+        acc3[c] = total
+        return carry
+
+    chunks = 2 * blocks
+    pl.semaphore_wait(barrier, quarter + 1)
+
+    def step(c, carry):
+        scale(2 * c + 1, scaled_b)
+        mix(2 * c, 0, scaled_a)
+        scale(jnp.minimum(2 * c + 2, 2 * chunks - 1), scaled_a)
+        mix(2 * c + 1, 1, scaled_b)
+        stage1(c)
+
+        @pl.when(c >= 1)
+        def _():
+            stage2(c - 1)
+
+        @pl.when(c >= 2)
+        def _():
+            stage3(c - 2)
+
+        return carry
+
+    lax.fori_loop(0, chunks, step, 0)
+    stage2(chunks - 1)
+    stage3(chunks - 2)
+    lax.fori_loop(0, blocks, stage4, 0)
+    up = acc3[:blocks].reshape(mag, wide)
+    left = jnp.dot(splitting, up, precision=HIGH, preferred_element_type=jnp.float32)
+    stage3(chunks - 1)
+    lax.fori_loop(blocks, chunks, stage4, 0)
 
     down = acc3[blocks:].reshape(mag, wide)
     turned = jnp.dot(down.T, splitting, precision=HIGH, preferred_element_type=jnp.float32)
@@ -341,12 +346,7 @@
     quarter = n // 4
     wide = 2 * mag
     assert offsets.shape[1] == n and n % 8 == 0 and mag % ROWS == 0
-    groups, first = [], 0
-    while first < chunks:
-        length = 2 if chunks - first > 3 else 1
-        groups.append((first, length))
-        first += length
-    sends = len(groups)
+    sends = chunks
     f32, bf16 = jnp.float32, jnp.bfloat16
     tile = (ROWS, wide)
     dma = pltpu.SemaphoreType.DMA
@@ -356,7 +356,7 @@
         for i, arg in enumerate(args)
     ]
     return pl.pallas_call(
-        functools.partial(kernel, n, groups),
+        functools.partial(kernel, n),
         out_shape=jax.ShapeDtypeStruct((1, atoms, atoms), f32),
         in_specs=[pl.BlockSpec(memory_space=pltpu.HBM)] * len(args),
         out_specs=pl.BlockSpec(memory_space=pltpu.VMEM),
@@ -371,16 +371,15 @@
             pltpu.VMEM((mag * slots, wide), f32),
             pltpu.VMEM((mag * slots, wide), f32),
             pltpu.VMEM((8 * n, 8 * slots), bf16),
-            pltpu.VMEM((2, ROWS * slots, 2 * norb), bf16),
+            pltpu.VMEM((8 * slots, 2 * norb), bf16),
+            pltpu.VMEM((8 * slots, 2 * norb), bf16),
             pltpu.VMEM((chunks, 2, 2, quarter) + tile, f32),
             pltpu.VMEM((chunks, quarter) + tile, f32),
             pltpu.VMEM((chunks,) + tile, f32),
-            pltpu.VMEM((chunks, 2, quarter) + tile, bf16),
-            pltpu.VMEM((chunks, 2, quarter) + tile, bf16),
-            pltpu.VMEM((chunks, quarter) + tile, bf16),
-            pltpu.VMEM((chunks, quarter) + tile, bf16),
-            pltpu.VMEM((quarter, chunks) + tile, bf16),
-            pltpu.VMEM((quarter - 1, chunks) + tile, bf16),
+            pltpu.VMEM((chunks, 2, quarter) + tile, f32),
+            pltpu.VMEM((chunks, quarter) + tile, f32),
+            pltpu.VMEM((chunks, quarter) + tile, f32),
+            pltpu.VMEM((chunks, quarter - 1) + tile, f32),
             dma((len(args),)),
             dma((sends,)),
             dma((sends,)),
@@ -390,7 +389,7 @@
             dma((sends, quarter - 1)),
         ],
         compiler_params=pltpu.CompilerParams(
-            collective_id=0, has_side_effects=True, vmem_limit_bytes=48 * 1024 * 1024
+            collective_id=0, has_side_effects=True, vmem_limit_bytes=63 * 1024 * 1024
         ),
     )(*args)
 

time: 33.6 us -> 33.7 us (level)
  Pallas kernels: 28 us -> 30.3 us
  local copies, waits for them, and re-layouts: 3.15 us -> 1.28 us
    pallas_call x1, Pallas kernels: 28 us -> 30.3 us  [local(): pl.pallas_call(functools.partial(kernel, n), out_shape=jax.ShapeDtypeStru...]
    unnamed x15 -> x1, local copies, waits for them, and re-layouts: 3.15 us -> 1.28 us
where the time goes in v3:
time: 33.7 us; the launch traced here: 33.5 us
  Pallas kernels  30.3 us (90%)
  between operations  1.95 us (6%)
  local copies, waits for them, and re-layouts  1.28 us (4%)
    pallas_call x1, Pallas kernels, local(): pl.pallas_call(functools.partial(kernel, n), out_shape=jax.ShapeDtypeStru...  30.3 us
    unnamed x1, local copies, waits for them, and re-layouts  1.28 us

profile of v3, /device:TPU:0, one launch (start us, length us, event | category | flops | bytes accessed | tf_op | source)
XLA Modules:
  0.0 33.5 jit_solution(6561694192636641815)
XLA Ops:
  1.9 30.3 %shard_map.100 = f32[1,8,8]{2,1,0:T(8,128)} custom-call(bf16[1,2,64,1024]{3,2,1,0:T(8,128)(2,1)} %vec_hbm.1, bf16[31,2,512]{2,1,0:T(2,128)(2,1)} %lev_hbm.1, bf16[3,31]{1,0:T(4,128)(2,1)} %k_hbm.1, s32[1]{0:T(128)S(6)} %copy.12.count_hbm, f32[1]{0:T(128)S(6)} %copy.13.er_hbm, f32[1]{0:T(128)S(6)} %copy.14.ei_hbm, s32[3,16]{1,0:T(4,128)} %off_hbm.1, ...), custom_call_target="tpu_custom_call" | custom-call | tf_op jit(solution)/shard_map/pallas_call | solution.py:358
  32.2 1.3 %copy.15 = f32[1,8,8]{2,1,0:T(8,128)} copy(f32[1,8,8]{2,1,0:T(8,128)} %shard_map.100) | data formatting | bytes 512

commit v4 on v3

--- a/solution.py
+++ b/solution.py
@@ -12,12 +12,22 @@
 
 ROWS = 16
 HIGH = lax.Precision.HIGHEST
+PIECE = 128
 ACROSS = (((1,), (1,)), ((), ()))
 
 
 def wave(turns):
-    part = (turns - jnp.round(turns)) * two_pi
-    return jnp.cos(part), jnp.sin(part)
+    def cosine(part):
+        part = part - jnp.round(part)
+        x = (0.25 - jnp.abs(part)) * two_pi
+        u = x * x
+        series = 1.0 / 6227020800.0
+        for term in (-1.0 / 39916800.0, 1.0 / 362880.0, -1.0 / 5040.0, 1.0 / 120.0, -1.0 / 6.0):
+            series = series * u + term
+        return x + x * (u * series)
+
+    turns = turns - jnp.round(turns)
+    return cosine(turns), cosine(turns - 0.25)
 
 
 def one_hot(condition):
@@ -60,8 +70,7 @@
     ctab,
     stab,
     wbd,
-    scaled_a,
-    scaled_b,
+    scaled,
     acc,
     acc2,
     acc3,
@@ -102,6 +111,7 @@
     slots = levels.shape[1]
     atoms = orb_ref.shape[0]
     blocks = mag // ROWS
+    pieces = norb // PIECE
     quarter, eighth = n // 4, n // 8
     wide = 2 * mag
 
@@ -134,10 +144,14 @@
         levels[spin, kslot:, :] = jnp.zeros((slots - kslot, norb), jnp.float32)
         vectors = vec_ref[0, spin]
         vf[spin] = vectors.astype(jnp.float32)
-        right[spin, :mag, :] = vectors
-        right[spin, mag:, :norb] = -vectors[:, norb:]
-        right[spin, mag:, norb:] = vectors[:, :norb]
-        flipped[spin] = right[spin].T
+        for t in range(pieces):
+            re_part = vectors[:, t * PIECE : (t + 1) * PIECE]
+            im_part = vectors[:, norb + t * PIECE : norb + (t + 1) * PIECE]
+            right[:mag, :PIECE] = re_part
+            right[:mag, PIECE:] = im_part
+            right[mag:, :PIECE] = -im_part
+            right[mag:, PIECE:] = re_part
+            flipped[spin, t] = right[...].T
         shift = er - levels[spin]
         denom = shift * shift + ei * ei
         inverse = 1.0 / denom
@@ -146,18 +160,6 @@
         return carry
 
     lax.fori_loop(0, 2, prepare, 0)
-
-    def scale(h, scaled):
-        spin, start = h // (2 * blocks), lax.rem(h, 2 * blocks) * 8
-        f_re, f_im = fre[spin], fim[spin]
-        for j in range(8):
-            v = vf[spin, pl.ds(start + j, 1), :]
-            v_re, v_im = v[:, :norb], v[:, norb:]
-            band = slice(j * slots, (j + 1) * slots)
-            scaled[band, :norb] = (v_re * f_re - v_im * f_im).astype(jnp.bfloat16)
-            scaled[band, norb:] = (v_re * f_im + v_im * f_re).astype(jnp.bfloat16)
-
-    scale(0, scaled_a)
 
     lane = iota((1, wide), 1)
     lane = jnp.where(lane >= mag, lane - mag, lane)
@@ -229,21 +231,36 @@
     member_rows = jnp.where(iota((atoms, mag), 0) == id_row[:, :mag], 1.0, 0.0)
     member_cols = jnp.where(id_col == iota((mag, atoms), 1), 1.0, 0.0)
 
-    def mix(h, part, scaled):
-        spin, start = h // (2 * blocks), lax.rem(h, 2 * blocks) * deep
-        bare = jnp.dot(scaled[...], flipped[spin], preferred_element_type=jnp.float32)
-        here = pl.ds(pl.multiple_of(start, deep), deep)
+    def compute(c):
+        spin, start = c // blocks, lax.rem(c, blocks) * ROWS
+        bare = None
+        for t in range(pieces):
+            at = slice(t * PIECE, (t + 1) * PIECE)
+            f_re, f_im = fre[spin, :, at], fim[spin, :, at]
+            mirror = slice(norb + t * PIECE, norb + (t + 1) * PIECE)
+            these = pl.ds(pl.multiple_of(start, ROWS), ROWS)
+            rows_re, rows_im = vf[spin, these, at], vf[spin, these, mirror]
+            for j in range(ROWS):
+                v_re, v_im = rows_re[j : j + 1], rows_im[j : j + 1]
+                band = slice(j * slots, (j + 1) * slots)
+                scaled[t, band, :PIECE] = (v_re * f_re - v_im * f_im).astype(jnp.bfloat16)
+                scaled[t, band, PIECE:] = (v_re * f_im + v_im * f_re).astype(jnp.bfloat16)
+            part = jnp.dot(scaled[t], flipped[spin, t], preferred_element_type=jnp.float32)
+            bare = part if t == 0 else bare + part
+        here = pl.ds(pl.multiple_of(start * slots, ROWS * slots), ROWS * slots)
         green = bare * ctab[here, :] + pltpu.roll(bare, mag, 1) * stab[here, :]
-        mixed = jnp.dot(
-            wbd[...], green.astype(jnp.bfloat16), preferred_element_type=jnp.float32
-        )
+        green = green.astype(jnp.bfloat16)
+        side = jnp.concatenate([green[:deep], green[deep:]], 1)
+        mixed = jnp.dot(wbd[...], side, preferred_element_type=jnp.float32)
         sense = jnp.where(spin == 0, 1.0, -1.0) * -sign
-        even = mixed[: 4 * n].reshape(2, 2, eighth, 8, wide)
-        odd = (pltpu.roll(mixed[4 * n :], mag, 1) * sense).reshape(2, 2, eighth, 8, wide)
-        rows = slice(part * 8, part * 8 + 8)
-        c = h // 2
-        acc[c, :, :, :eighth, rows, :] = even + odd
-        acc[c, :, :, eighth:, rows, :] = even - odd
+        for part in range(ROWS // 8):
+            half_mixed = mixed[:, part * wide : (part + 1) * wide]
+            even = half_mixed[: 4 * n].reshape(2, 2, eighth, 8, wide)
+            odd = pltpu.roll(half_mixed[4 * n :], mag, 1) * sense
+            odd = odd.reshape(2, 2, eighth, 8, wide)
+            rows = slice(part * 8, part * 8 + 8)
+            acc[c, :, :, :eighth, rows, :] = even + odd
+            acc[c, :, :, eighth:, rows, :] = even - odd
 
     def copy1(c):
         return pltpu.make_async_remote_copy(
@@ -304,10 +321,7 @@
     pl.semaphore_wait(barrier, quarter + 1)
 
     def step(c, carry):
-        scale(2 * c + 1, scaled_b)
-        mix(2 * c, 0, scaled_a)
-        scale(jnp.minimum(2 * c + 2, 2 * chunks - 1), scaled_a)
-        mix(2 * c + 1, 1, scaled_b)
+        compute(c)
         stage1(c)
 
         @pl.when(c >= 1)
@@ -347,6 +361,8 @@
     wide = 2 * mag
     assert offsets.shape[1] == n and n % 8 == 0 and mag % ROWS == 0
     sends = chunks
+    pieces = norb // PIECE
+    assert norb % PIECE == 0 and ROWS == 16
     f32, bf16 = jnp.float32, jnp.bfloat16
     tile = (ROWS, wide)
     dma = pltpu.SemaphoreType.DMA
@@ -363,16 +379,15 @@
         scratch_shapes=staged
         + [
             pltpu.VMEM((2, mag, 2 * norb), f32),
-            pltpu.VMEM((2, wide, 2 * norb), bf16),
-            pltpu.VMEM((2, 2 * norb, wide), bf16),
+            pltpu.VMEM((wide, 2 * PIECE), bf16),
+            pltpu.VMEM((2, pieces, 2 * PIECE, wide), bf16),
             pltpu.VMEM((2, slots, norb), f32),
             pltpu.VMEM((2, slots, norb), f32),
             pltpu.VMEM((2, slots, norb), f32),
             pltpu.VMEM((mag * slots, wide), f32),
             pltpu.VMEM((mag * slots, wide), f32),
             pltpu.VMEM((8 * n, 8 * slots), bf16),
-            pltpu.VMEM((8 * slots, 2 * norb), bf16),
-            pltpu.VMEM((8 * slots, 2 * norb), bf16),
+            pltpu.VMEM((pieces, ROWS * slots, 2 * PIECE), bf16),
             pltpu.VMEM((chunks, 2, 2, quarter) + tile, f32),
             pltpu.VMEM((chunks, quarter) + tile, f32),
             pltpu.VMEM((chunks,) + tile, f32),

time: 33.7 us -> 33.1 us (0.982)
  Pallas kernels: 30.3 us -> 29.6 us
    pallas_call x1, Pallas kernels: 30.3 us -> 29.6 us  [local(): pl.pallas_call(functools.partial(kernel, n), out_shape=jax.ShapeDtypeStru...]
where the time goes in v4:
time: 33.1 us; the launch traced here: 32.9 us
  Pallas kernels  29.6 us (89%)
  between operations  1.95 us (6%)
  local copies, waits for them, and re-layouts  1.28 us (4%)
    pallas_call x1, Pallas kernels, local(): pl.pallas_call(functools.partial(kernel, n), out_shape=jax.ShapeDtypeStru...  29.6 us
    unnamed x1, local copies, waits for them, and re-layouts  1.28 us

profile of v4, /device:TPU:0, one launch (start us, length us, event | category | flops | bytes accessed | tf_op | source)
XLA Modules:
  0.0 32.9 jit_solution(3845959459526163481)
XLA Ops:
  1.9 29.6 %shard_map.100 = f32[1,8,8]{2,1,0:T(8,128)} custom-call(bf16[1,2,64,1024]{3,2,1,0:T(8,128)(2,1)} %vec_hbm.1, bf16[31,2,512]{2,1,0:T(2,128)(2,1)} %lev_hbm.1, bf16[3,31]{1,0:T(4,128)(2,1)} %k_hbm.1, s32[1]{0:T(128)S(6)} %copy.12.count_hbm, f32[1]{0:T(128)S(6)} %copy.13.er_hbm, f32[1]{0:T(128)S(6)} %copy.14.ei_hbm, s32[3,16]{1,0:T(4,128)} %off_hbm.1, ...), custom_call_target="tpu_custom_call" | custom-call | tf_op jit(solution)/shard_map/pallas_call | solution.py:374
  31.6 1.3 %copy.15 = f32[1,8,8]{2,1,0:T(8,128)} copy(f32[1,8,8]{2,1,0:T(8,128)} %shard_map.100) | data formatting | bytes 512

commit v5 on v4

--- a/solution.py
+++ b/solution.py
@@ -324,17 +324,20 @@
         compute(c)
         stage1(c)
 
-        @pl.when(c >= 1)
-        def _():
-            stage2(c - 1)
-
         @pl.when(c >= 2)
         def _():
-            stage3(c - 2)
+            stage2(c - 2)
+
+        @pl.when(c >= 4)
+        def _():
+            stage3(c - 4)
 
         return carry
 
     lax.fori_loop(0, chunks, step, 0)
+    stage2(chunks - 2)
+    stage3(chunks - 4)
+    stage3(chunks - 3)
     stage2(chunks - 1)
     stage3(chunks - 2)
     lax.fori_loop(0, blocks, stage4, 0)

time: 33.1 us -> 31 us (0.937)
  Pallas kernels: 29.6 us -> 27.6 us
    pallas_call x1, Pallas kernels: 29.6 us -> 27.6 us  [local(): pl.pallas_call(functools.partial(kernel, n), out_shape=jax.ShapeDtypeStru...]
where the time goes in v5:
time: 31 us; the launch traced here: 30.8 us
  Pallas kernels  27.6 us (89%)
  between operations  1.95 us (6%)
  local copies, waits for them, and re-layouts  1.28 us (4%)
    pallas_call x1, Pallas kernels, local(): pl.pallas_call(functools.partial(kernel, n), out_shape=jax.ShapeDtypeStru...  27.6 us
    unnamed x1, local copies, waits for them, and re-layouts  1.28 us

profile of v5, /device:TPU:0, one launch (start us, length us, event | category | flops | bytes accessed | tf_op | source)
XLA Modules:
  0.0 30.8 jit_solution(15868172617562358)
XLA Ops:
  1.9 27.6 %shard_map.100 = f32[1,8,8]{2,1,0:T(8,128)} custom-call(bf16[1,2,64,1024]{3,2,1,0:T(8,128)(2,1)} %vec_hbm.1, bf16[31,2,512]{2,1,0:T(2,128)(2,1)} %lev_hbm.1, bf16[3,31]{1,0:T(4,128)(2,1)} %k_hbm.1, s32[1]{0:T(128)S(6)} %copy.12.count_hbm, f32[1]{0:T(128)S(6)} %copy.13.er_hbm, f32[1]{0:T(128)S(6)} %copy.14.ei_hbm, s32[3,16]{1,0:T(4,128)} %off_hbm.1, ...), custom_call_target="tpu_custom_call" | custom-call | tf_op jit(solution)/shard_map/pallas_call | solution.py:377
  29.5 1.3 %copy.15 = f32[1,8,8]{2,1,0:T(8,128)} copy(f32[1,8,8]{2,1,0:T(8,128)} %shard_map.100) | data formatting | bytes 512

commit v6 on v4

--- a/solution.py
+++ b/solution.py
@@ -328,13 +328,14 @@
         def _():
             stage2(c - 1)
 
-        @pl.when(c >= 2)
+        @pl.when(c >= 3)
         def _():
-            stage3(c - 2)
+            stage3(c - 3)
 
         return carry
 
     lax.fori_loop(0, chunks, step, 0)
+    stage3(chunks - 3)
     stage2(chunks - 1)
     stage3(chunks - 2)
     lax.fori_loop(0, blocks, stage4, 0)

time: 33.1 us -> 29.9 us (0.903)
  Pallas kernels: 29.6 us -> 26.5 us
    pallas_call x1, Pallas kernels: 29.6 us -> 26.5 us  [local(): pl.pallas_call(functools.partial(kernel, n), out_shape=jax.ShapeDtypeStru...]
where the time goes in v6:
time: 29.9 us; the launch traced here: 29.7 us
  Pallas kernels  26.5 us (89%)
  between operations  1.95 us (7%)
  local copies, waits for them, and re-layouts  1.28 us (4%)
    pallas_call x1, Pallas kernels, local(): pl.pallas_call(functools.partial(kernel, n), out_shape=jax.ShapeDtypeStru...  26.5 us
    unnamed x1, local copies, waits for them, and re-layouts  1.28 us

profile of v6, /device:TPU:0, one launch (start us, length us, event | category | flops | bytes accessed | tf_op | source)
XLA Modules:
  0.0 29.7 jit_solution(15187363977817613264)
XLA Ops:
  1.9 26.5 %shard_map.100 = f32[1,8,8]{2,1,0:T(8,128)} custom-call(bf16[1,2,64,1024]{3,2,1,0:T(8,128)(2,1)} %vec_hbm.1, bf16[31,2,512]{2,1,0:T(2,128)(2,1)} %lev_hbm.1, bf16[3,31]{1,0:T(4,128)(2,1)} %k_hbm.1, s32[1]{0:T(128)S(6)} %copy.12.count_hbm, f32[1]{0:T(128)S(6)} %copy.13.er_hbm, f32[1]{0:T(128)S(6)} %copy.14.ei_hbm, s32[3,16]{1,0:T(4,128)} %off_hbm.1, ...), custom_call_target="tpu_custom_call" | custom-call | tf_op jit(solution)/shard_map/pallas_call | solution.py:375
  28.5 1.3 %copy.15 = f32[1,8,8]{2,1,0:T(8,128)} copy(f32[1,8,8]{2,1,0:T(8,128)} %shard_map.100) | data formatting | bytes 512

commit v7 on v4

--- a/solution.py
+++ b/solution.py
@@ -328,14 +328,16 @@
         def _():
             stage2(c - 1)
 
-        @pl.when(c >= 2)
+        @pl.when(c >= 4)
         def _():
-            stage3(c - 2)
+            stage3(c - 4)
 
         return carry
 
     lax.fori_loop(0, chunks, step, 0)
     stage2(chunks - 1)
+    stage3(chunks - 4)
+    stage3(chunks - 3)
     stage3(chunks - 2)
     lax.fori_loop(0, blocks, stage4, 0)
     up = acc3[:blocks].reshape(mag, wide)

time: 33.1 us -> 28 us (0.85)
  Pallas kernels: 29.6 us -> 24.6 us
    pallas_call x1, Pallas kernels: 29.6 us -> 24.6 us  [local(): pl.pallas_call(functools.partial(kernel, n), out_shape=jax.ShapeDtypeStru...]
where the time goes in v7:
time: 28 us; the launch traced here: 27.8 us
  Pallas kernels  24.6 us (88%)
  between operations  1.95 us (7%)
  local copies, waits for them, and re-layouts  1.28 us (5%)
    pallas_call x1, Pallas kernels, local(): pl.pallas_call(functools.partial(kernel, n), out_shape=jax.ShapeDtypeStru...  24.6 us
    unnamed x1, local copies, waits for them, and re-layouts  1.28 us

profile of v7, /device:TPU:0, one launch (start us, length us, event | category | flops | bytes accessed | tf_op | source)
XLA Modules:
  0.0 27.8 jit_solution(10419682349979860569)
XLA Ops:
  1.9 24.6 %shard_map.100 = f32[1,8,8]{2,1,0:T(8,128)} custom-call(bf16[1,2,64,1024]{3,2,1,0:T(8,128)(2,1)} %vec_hbm.1, bf16[31,2,512]{2,1,0:T(2,128)(2,1)} %lev_hbm.1, bf16[3,31]{1,0:T(4,128)(2,1)} %k_hbm.1, s32[1]{0:T(128)S(6)} %copy.12.count_hbm, f32[1]{0:T(128)S(6)} %copy.13.er_hbm, f32[1]{0:T(128)S(6)} %copy.14.ei_hbm, s32[3,16]{1,0:T(4,128)} %off_hbm.1, ...), custom_call_target="tpu_custom_call" | custom-call | tf_op jit(solution)/shard_map/pallas_call | solution.py:376
  26.5 1.3 %copy.15 = f32[1,8,8]{2,1,0:T(8,128)} copy(f32[1,8,8]{2,1,0:T(8,128)} %shard_map.100) | data formatting | bytes 512

commit v8 on v7

--- a/solution.py
+++ b/solution.py
@@ -328,14 +328,15 @@
         def _():
             stage2(c - 1)
 
-        @pl.when(c >= 4)
+        @pl.when(c >= 5)
         def _():
-            stage3(c - 4)
+            stage3(c - 5)
 
         return carry
 
     lax.fori_loop(0, chunks, step, 0)
     stage2(chunks - 1)
+    stage3(chunks - 5)
     stage3(chunks - 4)
     stage3(chunks - 3)
     stage3(chunks - 2)

time: 28 us -> 28 us (level)
  no operation moved by 1% of the time
where the time goes in v8:
time: 28 us; the launch traced here: 27.8 us
  Pallas kernels  24.6 us (88%)
  between operations  1.95 us (7%)
  local copies, waits for them, and re-layouts  1.28 us (5%)
    pallas_call x1, Pallas kernels, local(): pl.pallas_call(functools.partial(kernel, n), out_shape=jax.ShapeDtypeStru...  24.6 us
    unnamed x1, local copies, waits for them, and re-layouts  1.28 us

profile of v8, /device:TPU:0, one launch (start us, length us, event | category | flops | bytes accessed | tf_op | source)
XLA Modules:
  0.0 27.8 jit_solution(14043593206506377686)
XLA Ops:
  1.9 24.6 %shard_map.100 = f32[1,8,8]{2,1,0:T(8,128)} custom-call(bf16[1,2,64,1024]{3,2,1,0:T(8,128)(2,1)} %vec_hbm.1, bf16[31,2,512]{2,1,0:T(2,128)(2,1)} %lev_hbm.1, bf16[3,31]{1,0:T(4,128)(2,1)} %k_hbm.1, s32[1]{0:T(128)S(6)} %copy.12.count_hbm, f32[1]{0:T(128)S(6)} %copy.13.er_hbm, f32[1]{0:T(128)S(6)} %copy.14.ei_hbm, s32[3,16]{1,0:T(4,128)} %off_hbm.1, ...), custom_call_target="tpu_custom_call" | custom-call | tf_op jit(solution)/shard_map/pallas_call | solution.py:377
  26.5 1.3 %copy.15 = f32[1,8,8]{2,1,0:T(8,128)} copy(f32[1,8,8]{2,1,0:T(8,128)} %shard_map.100) | data formatting | bytes 512
